TPU v7x, 32 devices: a whole 2x2x4 slice. The times are simulated.
32 devices in a mesh: groups: 2 (over y), dp: 8 (over z, x), tensor: 2 (over core).
Axes of the slice: x: 2, y: 2, z: 4, core: 2. Of those that a mesh axis runs over, the one named last changes fastest.
Arguments:
- tokens: bfloat16 [128, 8192], P(('groups', 'dp'), 'tensor'), parts along dimension 0, may hold values from -6 to 6
- request_adapter_index: int32 [128], P(('groups', 'dp')), parts along dimension 0, may hold values from 0 to 7
- adapter_storage_slot: int32 [16], P('groups'), parts along dimension 0, may hold values from 0 to 7, each once
- adapter_down_weight: bfloat16 [16, 32, 8192], P(('groups', 'dp'), None, 'tensor'), parts along dimension 0, may hold values from -0.0625 to 0.0625
- adapter_up_weight: bfloat16 [16, 32, 28672], P(('groups', 'dp'), None, 'tensor'), parts along dimension 0, may hold values from -1.5 to 1.5
- gate_projected_base: bfloat16 [128, 28672], P(('groups', 'dp'), 'tensor'), parts along dimension 0, may hold values from -6 to 6
- up_projected_base: bfloat16 [128, 28672], P(('groups', 'dp'), 'tensor'), parts along dimension 0, may hold values from -6 to 6
Outputs:
- hidden: bfloat16 [128, 28672], P(('groups', 'dp'), 'tensor'), parts along dimension 0
There are 2 independent parts, one for each index of `groups`. A program takes and returns all parts, laid end to end along the dimension named above; each array names one. Nothing has to cross between parts.
Inputs may be any that keep to these rules, and one draw needn't show every extreme that they name: `adapter_storage_slot`: each slot appears exactly once.
All inputs are finite; a program needn't handle non-finite values.
Results may differ from a plain program's by a relative error of at most 0.0062.
Values may be sent and summed in bfloat16 or wider, within the bound.
A program may use at most 64 MiB of HBM per device.

v0:
```python
import math

import jax
import jax.numpy as jnp
from jax import lax
from jax.sharding import PartitionSpec as P


def local(
    tokens,
    request_adapter_index,
    adapter_storage_slot,
    adapter_down_weight,
    adapter_up_weight,
    gate_projected_base,
    up_projected_base,
):
    holding_count, paired_rank, half_rank_width = adapter_down_weight.shape
    rank_size = paired_rank // 2
    ids_all = lax.all_gather(request_adapter_index, "dp", axis=0, tiled=True)
    total_rows = ids_all.shape[0]
    adapter_count = adapter_storage_slot.shape[0]
    id_match = ids_all[:, None] == jnp.arange(adapter_count, dtype=jnp.int32)[None, :]
    slot_all = jnp.sum(jnp.where(id_match, adapter_storage_slot[None, :], 0), axis=1)
    flattened_down = adapter_down_weight.reshape(holding_count * paired_rank, half_rank_width)
    owner_index = lax.axis_index("dp")
    shard_rows = lax.all_gather(tokens, "dp", axis=0, tiled=True)
    row_count = shard_rows.shape[0]
    projected = jnp.einsum(
        "md,cd->mc", shard_rows, flattened_down, preferred_element_type=jnp.float32
    )
    projected = projected.reshape(row_count, holding_count, paired_rank)
    local_slot = slot_all - owner_index * holding_count
    picker = (local_slot[:, None] == jnp.arange(holding_count, dtype=jnp.int32)[None, :]).astype(
        jnp.float32
    )
    term_rows = jnp.sum(projected * picker[:, :, None], axis=1)
    low_rank = lax.psum(term_rows, ("dp", "tensor"))
    low_bf = low_rank.astype(jnp.bfloat16)
    up_cols = lax.all_to_all(
        adapter_up_weight.reshape(holding_count * paired_rank, adapter_up_weight.shape[2]),
        "dp",
        split_axis=1,
        concat_axis=0,
        tiled=True,
    )
    narrow = up_cols.shape[1]
    up_four = up_cols.reshape(adapter_count, 2, rank_size, narrow)
    block_row_span = math.gcd(total_rows, 256)
    block_count = total_rows // block_row_span
    adapter_range = jnp.arange(adapter_count, dtype=jnp.int32)

    def expand(block_args):
        low_block, storage_slot_block = block_args
        onehot = (storage_slot_block[:, None] == adapter_range[None, :]).astype(jnp.bfloat16)
        spread = onehot[:, :, None, None] * low_block.reshape(block_row_span, 1, 2, rank_size)
        update = jnp.einsum("rajk,ajkf->rjf", spread, up_four, preferred_element_type=jnp.float32)
        return update.astype(jnp.bfloat16)

    deltas = lax.map(
        expand,
        (
            low_bf.reshape(block_count, block_row_span, paired_rank),
            slot_all.reshape(block_count, block_row_span),
        ),
    )
    deltas = deltas.reshape(total_rows, 2, narrow)
    home_rows = lax.all_to_all(deltas, "dp", split_axis=0, concat_axis=2, tiled=True)
    gate_sum = gate_projected_base.astype(jnp.float32) + home_rows[:, 0].astype(jnp.float32)
    up_sum = up_projected_base.astype(jnp.float32) + home_rows[:, 1].astype(jnp.float32)
    return (jax.nn.silu(gate_sum) * up_sum).astype(jnp.bfloat16)


def solution(mesh):
    in_specs = (
        P(("groups", "dp"), "tensor"),
        P(("groups", "dp")),
        P("groups"),
        P(("groups", "dp"), None, "tensor"),
        P(("groups", "dp"), None, "tensor"),
        P(("groups", "dp"), "tensor"),
        P(("groups", "dp"), "tensor"),
    )
    out_specs = P(("groups", "dp"), "tensor")
    return jax.shard_map(local, mesh=mesh, in_specs=in_specs, out_specs=out_specs, check_vma=False)
```

profile of v0, /device:TPU:0, one launch (start us, length us, event | category | flops | bytes accessed | tf_op | source)
XLA Modules:
  0.0 139.4 jit_solution(13796507168766610662)
XLA Ops:
  0.0 0.0 copy-start
  0.0 1.4 copy.20
  1.4 1.1 copy.15
  2.5 7.4 %all-to-all-start = ((bf16[32,8,1792]{2,0,1:T(8,128)(2,1)}), bf16[32,8,1792]{2,0,1:T(8,128)(2,1)S(1)}, u32[]{:S(2)}, u32[]{:S(2)}) async-start(bf16[32,8,1792]{2,0,1:T(8,128)(2,1)} %copy.15), calls=%async_computation | async-start | bytes 1835008 | tf_op jit(solution)/shard_map/all_to_all | solution.py:40
  9.9 0.7 copy-done.6
  10.5 0.6 dynamic-slice.2
  11.7 0.0 copy-start.4
  11.8 0.6 copy-done.4
  12.4 0.2 dynamic-update-slice
  12.6 20.5 %all-reduce = s32[64]{0:T(128)S(1)} all-reduce(s32[64]{0:T(128)S(1)} %dynamic-update-slice), channel_id=1, replica_groups=mesh['groups'=2,'dp'=8,'tensor'=2] {'dp'}, use_global_device_ids=true, to_apply=%add | all-reduce | flops 64 | bytes 512
  33.1 0.0 copy-done.5
  33.1 0.1 select_reduce_fusion
  33.2 0.0 copy-done.3
  33.2 31.3 %all_gather.7 = bf16[64,4096]{1,0:T(8,128)(2,1)S(1)} all-gather(bf16[8,4096]{1,0:T(8,128)(2,1)S(1)} %copy-done.3), channel_id=1, replica_groups=mesh['groups'=2,'dp'=8,'tensor'=2] {'dp'}, dimensions={0}, use_global_device_ids=true | all-gather | bytes 589824 | tf_op jit(solution)/shard_map/all_gather | solution.py:27
  64.5 0.0 copy-done
  64.5 0.3 convolution_multiply_fusion
  64.7 57.6 %psum.7 = bf16[64,32]{0,1:T(8,128)(2,1)S(1)} all-reduce(f32[64,32]{0,1:T(8,128)S(1)} %convolution_multiply_fusion), channel_id=1, replica_groups=mesh['groups'=2,'dp'=8,'tensor'=2] {'dp','tensor'}, use_global_device_ids=true, to_apply=%region_1.2 | all-reduce | flops 2048 | bytes 12288 | tf_op jit(solution)/shard_map/psum | solution.py:38
  122.3 0.0 all-to-all-done
  122.4 0.3 fusion.1
  122.7 0.5 copy.17
  123.2 14.3 %all_to_all.34 = bf16[64,2,1792]{2,1,0:T(2,128)(2,1)S(1)} all-to-all(bf16[64,2,1792]{2,1,0:T(2,128)(2,1)S(1)} %copy.17), channel_id=1, replica_groups=mesh['groups'=2,'dp'=8,'tensor'=2] {'dp'}, dimensions={0} | all-to-all | bytes 917504 | tf_op jit(solution)/shard_map/all_to_all | solution.py:68
  137.5 0.9 copy-done.1
  138.4 0.1 copy-done.2
  138.5 0.9 fusion.4
  (9 shorter events, 0.1 us)
Async XLA Ops:
  0.0 64.5 %copy-start = (bf16[1,32,4096]{2,1,0:T(8,128)(2,1)S(1)}, bf16[1,32,4096]{2,1,0:T(8,128)(2,1)}, u32[]{:S(2)}) copy-start(bf16[1,32,4096]{2,1,0:T(8,128)(2,1)} %param.10) | copy-start | bytes 786436
  2.5 30.7 %copy-start.3 = (bf16[8,4096]{1,0:T(8,128)(2,1)S(1)}, bf16[8,4096]{1,0:T(8,128)(2,1)}, u32[]{:S(2)}) copy-start(bf16[8,4096]{1,0:T(8,128)(2,1)} %param.7) | copy-start | bytes 196612
  2.5 119.9 %all-to-all-start = ((bf16[32,8,1792]{2,0,1:T(8,128)(2,1)}), bf16[32,8,1792]{2,0,1:T(8,128)(2,1)S(1)}, u32[]{:S(2)}, u32[]{:S(2)}) async-start(bf16[32,8,1792]{2,0,1:T(8,128)(2,1)} %copy.15), calls=%async_computation | async-start | bytes 1835008 | tf_op jit(solution)/shard_map/all_to_all | solution.py:40
  9.8 0.7 copy-start.6
  11.7 0.7 copy-start.4
  12.6 20.5 %copy-start.5 = (s32[8]{0:T(128)S(1)}, s32[8]{0:T(128)}, u32[]{:S(2)}) copy-start(s32[8]{0:T(128)} %param.9) | copy-start | bytes 100
  137.5 0.9 copy-start.1
  137.5 1.0 copy-start.2
where the time goes:
time: 140 us; the launch traced here: 139 us
  blocking collectives  124 us (89%)
  starting transfers between devices  7.38 us (5%)
  local copies, waits for them, and re-layouts  6.05 us (4%)
    psum x1, blocking collectives, local(): low_rank = lax.psum(term_rows, ('dp', 'tensor'))  57.6 us
    all_gather x1, blocking collectives, local(): shard_rows = lax.all_gather(tokens, 'dp', axis=0, tiled=True)  31.3 us
    unnamed x1, blocking collectives  20.5 us
    all_to_all x1, blocking collectives, local(): lax.all_to_all(deltas, 'dp', split_axis=0, concat_axis=2, tiled=True)  14.3 us
    all_to_all x1, starting transfers between devices, local(): lax.all_to_all(adapter_up_weight.reshape(holding_count * paired_rank, ada...  7.38 us
    unnamed x18, local copies, waits for them, and re-layouts  4.44 us
  transfers between devices with their start and end apart: 1, of which 0 were waited for; matrix products, arithmetic and copies ran while one was open for 1% of the time, Pallas kernels for 0%

commit v1 on v0

--- a/solution.py
+++ b/solution.py
@@ -1,12 +1,15 @@
+import functools
 import math
 
 import jax
 import jax.numpy as jnp
 from jax import lax
+from jax.experimental import pallas as pl
+from jax.experimental.pallas import tpu as pltpu
 from jax.sharding import PartitionSpec as P
 
 
-def local(
+def plain(
     tokens,
     request_adapter_index,
     adapter_storage_slot,
@@ -71,6 +74,291 @@
     return (jax.nn.silu(gate_sum) * up_sum).astype(jnp.bfloat16)
 
 
+MESH = pl.DeviceIdType.MESH
+LANES = 128
+
+
+def kernel(
+    n,
+    parts,
+    ids,
+    storage,
+    tokens,
+    down,
+    up,
+    gate_base,
+    up_base,
+    out,
+    tok_send,
+    tok_all,
+    pair_send,
+    pair_recv,
+    low_all,
+    up_all,
+    delta_send,
+    delta_recv,
+    gate_vmem,
+    up_vmem,
+    tok_ssem,
+    tok_rsem,
+    pair_sem,
+    low_ssem,
+    low_rsem,
+    up_ssem,
+    up_rsem,
+    delta_ssem,
+    delta_rsem,
+    local_sem,
+):
+    group = lax.axis_index("groups")
+    me = lax.axis_index("dp")
+    core = lax.axis_index("tensor")
+    rows, width = tokens.shape
+    half = width // 2
+    pair_rank = down.shape[0]
+    narrow = up_all.shape[2]
+    total = n * rows
+
+    def at(peer):
+        return (group, peer, core)
+
+    peers = [lax.rem(me + step, n) for step in range(1, n)]
+
+    barrier = pltpu.get_barrier_semaphore()
+    for peer in peers:
+        pl.semaphore_signal(barrier, inc=1, device_id=at(peer), device_id_type=MESH)
+    pl.semaphore_signal(barrier, inc=1, device_id=(group, me, 1 - core), device_id_type=MESH)
+
+    bases = [
+        pltpu.make_async_copy(gate_base, gate_vmem, local_sem.at[0]),
+        pltpu.make_async_copy(up_base, up_vmem, local_sem.at[1]),
+    ]
+    own_columns = pl.ds(pl.multiple_of(me * narrow, LANES), narrow)
+    own_up = pltpu.make_async_copy(up.at[:, own_columns], up_all.at[me], local_sem.at[2])
+    own_up.start()
+    for copy in bases:
+        copy.start()
+
+    slot_rows = lax.broadcasted_iota(jnp.int32, (rows, LANES), 0)
+    slots = jnp.zeros((rows, LANES), jnp.int32)
+    for row in range(rows):
+        slots = jnp.where(slot_rows == row, storage[ids[row]], slots)
+    slots = slots.astype(jnp.float32)
+    values = tokens[...].astype(jnp.float32)
+    packed = jnp.concatenate(
+        [
+            jnp.concatenate([values[:, :half], slots], axis=1),
+            jnp.concatenate([values[:, half:], slots], axis=1),
+        ],
+        axis=0,
+    ).astype(jnp.bfloat16)
+    tok_send[...] = packed
+    tok_all[me] = packed
+
+    pl.semaphore_wait(barrier, n)
+
+    def tok_copy(peer, slot_at, sem_at):
+        return pltpu.make_async_remote_copy(
+            src_ref=tok_send,
+            dst_ref=tok_all.at[slot_at],
+            send_sem=tok_ssem.at[peer],
+            recv_sem=tok_rsem.at[sem_at],
+            device_id=at(peer),
+            device_id_type=MESH,
+        )
+
+    def up_copy(peer, slot_at, part):
+        start, size = parts[part]
+        columns = pl.ds(pl.multiple_of(peer * narrow + start, LANES), size)
+        return pltpu.make_async_remote_copy(
+            src_ref=up.at[:, columns],
+            dst_ref=up_all.at[slot_at, :, pl.ds(start, size)],
+            send_sem=up_ssem.at[peer, part],
+            recv_sem=up_rsem.at[slot_at, part],
+            device_id=at(peer),
+            device_id_type=MESH,
+        )
+
+    def low_copy(peer, slot_at):
+        return pltpu.make_async_remote_copy(
+            src_ref=low_all.at[me],
+            dst_ref=low_all.at[slot_at],
+            send_sem=low_ssem.at[peer],
+            recv_sem=low_rsem.at[slot_at],
+            device_id=at(peer),
+            device_id_type=MESH,
+        )
+
+    def delta_copy(peer, slot_at, part):
+        start, size = parts[part]
+        columns = pl.ds(start, size)
+        return pltpu.make_async_remote_copy(
+            src_ref=delta_send.at[peer, :, columns],
+            dst_ref=delta_recv.at[slot_at, :, columns],
+            send_sem=delta_ssem.at[peer, part],
+            recv_sem=delta_rsem.at[slot_at, part],
+            device_id=at(peer),
+            device_id_type=MESH,
+        )
+
+    for peer in peers:
+        tok_copy(peer, me, me).start()
+    for part in range(len(parts)):
+        for peer in peers:
+            up_copy(peer, me, part).start()
+
+    repeat = LANES // pair_rank
+    first, second = down[:, :half], down[:, half:]
+    weights = jnp.concatenate([first] * repeat + [second] * repeat, axis=0)
+    for peer in peers:
+        tok_copy(peer, peer, peer).wait_recv()
+    arrived = tok_all[...]
+    product = lax.dot_general(
+        arrived[:, :, :half].reshape(total * 2, half),
+        weights,
+        (((1,), (1,)), ((), ())),
+        preferred_element_type=jnp.float32,
+    ).reshape(n, 2, rows, 2 * LANES)
+    slot_of = arrived[:, :, half:].astype(jnp.float32).reshape(n, 2, rows, LANES)[:, 0]
+    lane_group = lax.broadcasted_iota(jnp.int32, (n, rows, LANES), 2) // pair_rank
+    mine = (slot_of == me.astype(jnp.float32)) & (lane_group == lax.rem(me, repeat))
+    low = product[:, 0, :, :LANES] + product[:, 1, :, LANES:]
+    low = jnp.where(mine, low, 0.0).reshape(total, LANES)
+    pair_send[...] = low
+    pair = pltpu.make_async_remote_copy(
+        src_ref=pair_send,
+        dst_ref=pair_recv,
+        send_sem=pair_sem.at[0],
+        recv_sem=pair_sem.at[1],
+        device_id=(group, me, 1 - core),
+        device_id_type=MESH,
+    )
+    pair.start()
+    pair.wait_recv()
+    low_all[me] = (low + pair_recv[...]).astype(jnp.bfloat16)
+    for peer in peers:
+        low_copy(peer, me).start()
+    for peer in peers:
+        low_copy(peer, peer).wait_recv()
+
+    codes = low_all[...].astype(jnp.float32)
+    groups = [
+        sum(codes[start + k] for k in range(repeat)) for start in range(0, n, repeat)
+    ]
+    spread = jnp.concatenate(groups, axis=1).reshape(n, rows, n * pair_rank)
+    lane = lax.broadcasted_iota(jnp.int32, spread.shape, 2)
+    is_gate = lax.rem(lane, pair_rank) < pair_rank // 2
+    spread = jnp.stack(
+        [jnp.where(is_gate, spread, 0.0), jnp.where(is_gate, 0.0, spread)], axis=1
+    )
+    spread = spread.reshape(2 * total, n * pair_rank).astype(jnp.bfloat16)
+
+    own_up.wait()
+    for part, (start, size) in enumerate(parts):
+        for peer in peers:
+            up_copy(peer, peer, part).wait_recv()
+        columns = pl.ds(start, size)
+        delta = jnp.dot(
+            spread,
+            up_all[:, :, columns].reshape(n * pair_rank, size),
+            preferred_element_type=jnp.float32,
+        )
+        delta_send[:, :, columns] = delta.astype(jnp.bfloat16).reshape(n, 2 * rows, size)
+        for peer in peers:
+            delta_copy(peer, me, part).start()
+
+    for copy in bases:
+        copy.wait()
+
+    def finish(source, part, block):
+        start, size = parts[part]
+        columns = pl.ds(pl.multiple_of(source * narrow + start, LANES), size)
+        block = block.astype(jnp.float32)
+        gate = gate_vmem[:, columns].astype(jnp.float32) + block[:rows]
+        raised = up_vmem[:, columns].astype(jnp.float32) + block[rows:]
+        out[:, columns] = (jax.nn.silu(gate) * raised).astype(out.dtype)
+
+    for part, (start, size) in enumerate(parts):
+        finish(me, part, delta_send[me, :, pl.ds(start, size)])
+        for peer in peers:
+            delta_copy(peer, peer, part).wait_recv()
+            finish(peer, part, delta_recv[peer, :, pl.ds(start, size)])
+
+    pair.wait_send()
+    for peer in peers:
+        tok_copy(peer, me, me).wait_send()
+        low_copy(peer, me).wait_send()
+        for part in range(len(parts)):
+            up_copy(peer, me, part).wait_send()
+            delta_copy(peer, me, part).wait_send()
+
+
+def cut(narrow, pieces):
+    tiles = narrow // LANES
+    edges = [tiles * k // pieces * LANES for k in range(pieces + 1)]
+    return tuple((a, b - a) for a, b in zip(edges, edges[1:]) if b > a)
+
+
+def local(mesh, *arrays):
+    tokens, ids, storage, down, up, gate_base, up_base = arrays
+    n = mesh.shape["dp"]
+    rows, width = tokens.shape
+    held, pair_rank, _ = down.shape
+    hidden = up.shape[2]
+    fits = (
+        held == 1
+        and mesh.shape["tensor"] == 2
+        and hidden % (n * LANES) == 0
+        and rows == 8
+        and width % (2 * LANES) == 0
+        and pair_rank % 16 == 0
+        and LANES % pair_rank == 0
+        and (n * pair_rank) % LANES == 0
+        and n <= 8
+    )
+    if not fits:
+        return plain(*arrays)
+    narrow = hidden // n
+    parts = cut(narrow, 2)
+    count = len(parts)
+    vmem = pl.BlockSpec(memory_space=pltpu.VMEM)
+    smem = pl.BlockSpec(memory_space=pltpu.SMEM)
+    hbm = pl.BlockSpec(memory_space=pl.ANY)
+    dma = pltpu.SemaphoreType.DMA
+    bf16 = jnp.bfloat16
+    return pl.pallas_call(
+        functools.partial(kernel, n, parts),
+        out_shape=jax.ShapeDtypeStruct((rows, hidden), bf16),
+        in_specs=[smem, smem, vmem, vmem, hbm, hbm, hbm],
+        out_specs=vmem,
+        scratch_shapes=[
+            pltpu.VMEM((2 * rows, width // 2 + LANES), bf16),
+            pltpu.VMEM((n, 2 * rows, width // 2 + LANES), bf16),
+            pltpu.VMEM((n * rows, LANES), jnp.float32),
+            pltpu.VMEM((n * rows, LANES), jnp.float32),
+            pltpu.VMEM((n, n * rows, LANES), bf16),
+            pltpu.VMEM((n, pair_rank, narrow), bf16),
+            pltpu.VMEM((n, 2 * rows, narrow), bf16),
+            pltpu.VMEM((n, 2 * rows, narrow), bf16),
+            pltpu.VMEM((rows, hidden), bf16),
+            pltpu.VMEM((rows, hidden), bf16),
+            dma((n,)),
+            dma((n,)),
+            dma((2,)),
+            dma((n,)),
+            dma((n,)),
+            dma((n, count)),
+            dma((n, count)),
+            dma((n, count)),
+            dma((n, count)),
+            dma((3,)),
+        ],
+        compiler_params=pltpu.CompilerParams(
+            collective_id=0, has_side_effects=True, vmem_limit_bytes=32 * 1024 * 1024
+        ),
+    )(ids, storage, tokens, down[0], up[0], gate_base, up_base)
+
+
 def solution(mesh):
     in_specs = (
         P(("groups", "dp"), "tensor"),
@@ -82,4 +370,4 @@
         P(("groups", "dp"), "tensor"),
     )
     out_specs = P(("groups", "dp"), "tensor")
-    return jax.shard_map(local, mesh=mesh, in_specs=in_specs, out_specs=out_specs, check_vma=False)
+    return jax.shard_map(functools.partial(local, mesh), mesh=mesh, in_specs=in_specs, out_specs=out_specs, check_vma=False)

time: 140 us -> 59.9 us (0.43)
  blocking collectives: 124 us -> 0 us
  Pallas kernels: 0 us -> 53.4 us
  starting transfers between devices: 7.38 us -> 0 us
    psum x1 -> x0, blocking collectives: 57.6 us -> none  [local(): low_rank = lax.psum(term_rows, ('dp', 'tensor'))]
    pallas_call x0 -> x1, Pallas kernels: none -> 53.4 us  [local(): pl.pallas_call(functools.partial(kernel, n, parts), out_shape=jax.ShapeDt...]
    all_gather x1 -> x0, blocking collectives: 31.3 us -> none  [local(): shard_rows = lax.all_gather(tokens, 'dp', axis=0, tiled=True)]
    unnamed x1 -> x0, blocking collectives: 20.5 us -> none
    all_to_all x1 -> x0, blocking collectives: 14.3 us -> none  [local(): lax.all_to_all(deltas, 'dp', split_axis=0, concat_axis=2, tiled=True)]
    all_to_all x1 -> x0, starting transfers between devices: 7.38 us -> none  [local(): lax.all_to_all(adapter_up_weight.reshape(holding_count * paired_rank, ada...]
    unnamed x18 -> x15, local copies, waits for them, and re-layouts: 4.44 us -> 6.2 us
  transfers between devices with their start and end apart: 1 -> 0, of which waited for: 0 -> 0; matrix products, arithmetic and copies ran while one was open for 1% -> 0% of each run, Pallas kernels for 0% -> 0%
where the time goes in v1:
time: 59.9 us; the launch traced here: 59.6 us
  Pallas kernels  53.4 us (89%)
  local copies, waits for them, and re-layouts  6.2 us (10%)
    pallas_call x1, Pallas kernels, local(): pl.pallas_call(functools.partial(kernel, n, parts), out_shape=jax.ShapeDt...  53.4 us
    unnamed x15, local copies, waits for them, and re-layouts  6.2 us

profile of v1, /device:TPU:0, one launch (start us, length us, event | category | flops | bytes accessed | tf_op | source)
XLA Modules:
  0.0 59.6 jit_solution(7287189919299893457)
XLA Ops:
  0.0 0.0 copy-start.5
  0.0 0.0 copy-start.6
  0.0 0.7 %copy-done.5 = s32[8]{0:T(128)S(1)} copy-done((s32[8]{0:T(128)S(1)}, s32[8]{0:T(128)}, u32[]{:S(2)}) %copy-start.5) | copy-done | bytes 56
  0.7 0.0 copy-done.6
  0.7 0.0 copy-start
  0.7 1.2 %copy-done = bf16[1,32,14336]{2,1,0:T(8,128)(2,1)S(1)} copy-done((bf16[1,32,14336]{2,1,0:T(8,128)(2,1)S(1)}, bf16[1,32,14336]{2,1,0:T(8,128)(2,1)}, u32[]{:S(2)}) %copy-start) | copy-done | bytes 917528
  1.9 0.0 copy-start.1
  1.9 0.9 %copy-done.1 = bf16[1,32,4096]{2,1,0:T(8,128)(2,1)S(1)} copy-done((bf16[1,32,4096]{2,1,0:T(8,128)(2,1)S(1)}, bf16[1,32,4096]{2,1,0:T(8,128)(2,1)}, u32[]{:S(2)}) %copy-start.1) | copy-done | bytes 262168
  2.8 0.0 copy-start.2
  2.8 0.9 %copy-done.2 = bf16[8,14336]{1,0:T(8,128)(2,1)S(1)} copy-done((bf16[8,14336]{1,0:T(8,128)(2,1)S(1)}, bf16[8,14336]{1,0:T(8,128)(2,1)}, u32[]{:S(2)}) %copy-start.2) | copy-done | bytes 229400
  3.7 0.0 copy-start.3
  3.7 0.9 %copy-done.3 = bf16[8,14336]{1,0:T(8,128)(2,1)S(1)} copy-done((bf16[8,14336]{1,0:T(8,128)(2,1)S(1)}, bf16[8,14336]{1,0:T(8,128)(2,1)}, u32[]{:S(2)}) %copy-start.3) | copy-done | bytes 229400
  4.7 0.0 copy-start.4
  4.7 0.8 %copy-done.4 = bf16[8,4096]{1,0:T(8,128)(2,1)S(1)} copy-done((bf16[8,4096]{1,0:T(8,128)(2,1)S(1)}, bf16[8,4096]{1,0:T(8,128)(2,1)}, u32[]{:S(2)}) %copy-start.4) | copy-done | bytes 65560
  5.5 53.4 %shard_map.73 = bf16[8,14336]{1,0:T(8,128)(2,1)S(1)} custom-call(s32[8]{0:T(128)S(1)} %copy-done.5, s32[8]{0:T(128)S(1)} %copy-done.6, bf16[8,4096]{1,0:T(8,128)(2,1)S(1)} %copy-done.4, bf16[32,4096]{1,0:T(8,128)(2,1)S(1)} %bitcast.3, bf16[32,14336]{1,0:T(8,128)(2,1)S(1)} %bitcast.2, bf16[8,14336]{1,0:T(8,128)(2,1)S(1)} %copy-done.2, ...), custom_call_target="tpu_custom_call" | custom-call | tf_op jit(solution)/shard_map/pallas_call | solution.py:329
  58.9 0.7 %copy.9 = bf16[8,14336]{1,0:T(8,128)(2,1)} copy(bf16[8,14336]{1,0:T(8,128)(2,1)S(1)} %shard_map.73) | data formatting | bytes 458752
Async XLA Ops:
  0.0 0.7 %copy-start.5 = (s32[8]{0:T(128)S(1)}, s32[8]{0:T(128)}, u32[]{:S(2)}) copy-start(s32[8]{0:T(128)} %ids.1) | copy-start | bytes 100
  0.0 0.7 %copy-start.6 = (s32[8]{0:T(128)S(1)}, s32[8]{0:T(128)}, u32[]{:S(2)}) copy-start(s32[8]{0:T(128)} %storage.1) | copy-start | bytes 100
  0.7 1.2 %copy-start = (bf16[1,32,14336]{2,1,0:T(8,128)(2,1)S(1)}, bf16[1,32,14336]{2,1,0:T(8,128)(2,1)}, u32[]{:S(2)}) copy-start(bf16[1,32,14336]{2,1,0:T(8,128)(2,1)} %param.11) | copy-start | bytes 2752516
  1.9 0.9 %copy-start.1 = (bf16[1,32,4096]{2,1,0:T(8,128)(2,1)S(1)}, bf16[1,32,4096]{2,1,0:T(8,128)(2,1)}, u32[]{:S(2)}) copy-start(bf16[1,32,4096]{2,1,0:T(8,128)(2,1)} %param.10) | copy-start | bytes 786436
  2.8 0.9 %copy-start.2 = (bf16[8,14336]{1,0:T(8,128)(2,1)S(1)}, bf16[8,14336]{1,0:T(8,128)(2,1)}, u32[]{:S(2)}) copy-start(bf16[8,14336]{1,0:T(8,128)(2,1)} %gate_base.1) | copy-start | bytes 688132
  3.7 0.9 %copy-start.3 = (bf16[8,14336]{1,0:T(8,128)(2,1)S(1)}, bf16[8,14336]{1,0:T(8,128)(2,1)}, u32[]{:S(2)}) copy-start(bf16[8,14336]{1,0:T(8,128)(2,1)} %up_base.1) | copy-start | bytes 688132
  4.7 0.8 %copy-start.4 = (bf16[8,4096]{1,0:T(8,128)(2,1)S(1)}, bf16[8,4096]{1,0:T(8,128)(2,1)}, u32[]{:S(2)}) copy-start(bf16[8,4096]{1,0:T(8,128)(2,1)} %tokens.1) | copy-start | bytes 196612

commit v2 on v0

--- a/solution.py
+++ b/solution.py
@@ -1,12 +1,15 @@
+import functools
 import math
 
 import jax
 import jax.numpy as jnp
 from jax import lax
+from jax.experimental import pallas as pl
+from jax.experimental.pallas import tpu as pltpu
 from jax.sharding import PartitionSpec as P
 
 
-def local(
+def plain(
     tokens,
     request_adapter_index,
     adapter_storage_slot,
@@ -71,6 +74,405 @@
     return (jax.nn.silu(gate_sum) * up_sum).astype(jnp.bfloat16)
 
 
+MESH = pl.DeviceIdType.MESH
+LANES = 128
+
+
+def kernel(
+    n,
+    parts,
+    ids,
+    storage,
+    tokens,
+    down,
+    up,
+    gate_base,
+    up_base,
+    out,
+    tok_vmem,
+    tok_send,
+    tok_all,
+    down_all,
+    sum_send,
+    sum_recv,
+    codes,
+    wide_up,
+    near_up,
+    wide_send,
+    near_send,
+    wide_recv,
+    near_recv,
+    gate_vmem,
+    up_vmem,
+    tok_ssem,
+    tok_rsem,
+    down_ssem,
+    down_rsem,
+    sum_ssem,
+    sum_rsem,
+    code_ssem,
+    code_rsem,
+    wide_ssem,
+    wide_rsem,
+    near_ssem,
+    near_rsem,
+    back_ssem,
+    back_rsem,
+    local_sem,
+):
+    group = lax.axis_index("groups")
+    me = lax.axis_index("dp")
+    core = lax.axis_index("tensor")
+    m = n // 2
+    side, place = me // m, lax.rem(me, m)
+    seat = place * 2 + core
+    rows, width = tok_vmem.shape
+    piece = width // m
+    bit = piece // 2
+    pair_rank = down.shape[0]
+    wide, near = wide_up.shape[2], near_up.shape[2]
+    wide_total = n * wide
+    total = n * rows
+
+    def remote(src, dst, send, recv, peer, peer_core=core):
+        return pltpu.make_async_remote_copy(
+            src_ref=src,
+            dst_ref=dst,
+            send_sem=send,
+            recv_sem=recv,
+            device_id=(group, peer, peer_core),
+            device_id_type=MESH,
+        )
+
+    across = [(1 - side) * m + lax.rem(place + step, m) for step in range(m)]
+    beside = [side * m + lax.rem(place + step, m) for step in range(1, m)]
+    peers = across + beside
+    seats = [lax.rem(seat + step, n) for step in range(1, n)]
+
+    tok_load = pltpu.make_async_copy(tokens, tok_vmem, local_sem.at[0])
+    tok_load.start()
+    barrier = pltpu.get_barrier_semaphore()
+    for peer in peers:
+        for peer_core in range(2):
+            pl.semaphore_signal(
+                barrier, inc=1, device_id=(group, peer, peer_core), device_id_type=MESH
+            )
+    pl.semaphore_signal(barrier, inc=1, device_id=(group, me, 1 - core), device_id_type=MESH)
+
+    def span(start, size):
+        return pl.ds(pl.multiple_of(start, LANES), size)
+
+    loads = [
+        pltpu.make_async_copy(down.at[:, span(place * piece, piece)], down_all.at[place], local_sem.at[1]),
+        pltpu.make_async_copy(up.at[:, span(me * wide, wide)], wide_up.at[me], local_sem.at[2]),
+        pltpu.make_async_copy(
+            up.at[:, span(wide_total + place * near, near)], near_up.at[place], local_sem.at[3]
+        ),
+        pltpu.make_async_copy(gate_base, gate_vmem, local_sem.at[4]),
+        pltpu.make_async_copy(up_base, up_vmem, local_sem.at[5]),
+    ]
+    for copy in loads:
+        copy.start()
+
+    slot_rows = lax.broadcasted_iota(jnp.int32, (rows, LANES), 0)
+    slots = jnp.zeros((rows, LANES), jnp.int32)
+    for row in range(rows):
+        slots = jnp.where(slot_rows == row, storage[ids[row]], slots)
+    slots = slots.astype(jnp.float32)
+    tok_load.wait()
+    values = tok_vmem[...].astype(jnp.float32)
+    for part in range(m):
+        cut_at = part * piece
+        tok_send[part] = jnp.concatenate(
+            [
+                jnp.concatenate([values[:, cut_at : cut_at + bit], slots], axis=1),
+                jnp.concatenate([values[:, cut_at + bit : cut_at + piece], slots], axis=1),
+            ],
+            axis=0,
+        ).astype(jnp.bfloat16)
+    tok_all[me] = tok_send[place]
+
+    pl.semaphore_wait(barrier, 2 * n - 1)
+
+    def tok_copy(peer, index):
+        return remote(
+            tok_send.at[lax.rem(peer, m)], tok_all.at[index], tok_ssem.at[peer], tok_rsem.at[index], peer
+        )
+
+    def down_copy(peer, index):
+        spot = lax.rem(peer, m)
+        return remote(
+            down.at[:, span(spot * piece, piece)],
+            down_all.at[index],
+            down_ssem.at[spot],
+            down_rsem.at[index],
+            peer,
+        )
+
+    def wide_copy(peer, index):
+        return remote(
+            up.at[:, span(peer * wide, wide)],
+            wide_up.at[index],
+            wide_ssem.at[peer],
+            wide_rsem.at[index],
+            peer,
+        )
+
+    def near_copy(peer, index):
+        spot = lax.rem(peer, m)
+        return remote(
+            up.at[:, span(wide_total + spot * near, near)],
+            near_up.at[index],
+            near_ssem.at[spot],
+            near_rsem.at[index],
+            peer,
+        )
+
+    def sum_copy(other, index):
+        return remote(
+            sum_send.at[other],
+            sum_recv.at[index],
+            sum_ssem.at[other],
+            sum_rsem.at[index],
+            side * m + other // 2,
+            lax.rem(other, 2),
+        )
+
+    def code_copy(peer, peer_core, code_side, code_seat):
+        return remote(
+            codes.at[side, seat],
+            codes.at[code_side, code_seat],
+            code_ssem.at[peer, peer_core],
+            code_rsem.at[code_side, code_seat],
+            peer,
+            peer_core,
+        )
+
+    def back_copy(peer, index, which):
+        kind, start, size = parts[which]
+        send, recv = (near_send, near_recv) if kind else (wide_send, wide_recv)
+        columns = pl.ds(start, size)
+        return remote(
+            send.at[peer, :, columns],
+            recv.at[index, :, columns],
+            back_ssem.at[peer, which],
+            back_rsem.at[index, which],
+            peer,
+        )
+
+    for peer in peers:
+        tok_copy(peer, me).start()
+    for peer in beside:
+        down_copy(peer, place).start()
+    for peer in across:
+        wide_copy(peer, me).start()
+    for peer in beside:
+        near_copy(peer, place).start()
+    for peer in beside:
+        wide_copy(peer, me).start()
+
+    loads[0].wait()
+    for peer in beside:
+        down_copy(peer, lax.rem(peer, m)).wait_recv()
+    for peer in peers:
+        tok_copy(peer, peer).wait_recv()
+    arrived = tok_all[...]
+    held = down_all[...].reshape(m * pair_rank, piece)
+    product = lax.dot_general(
+        arrived[:, :, :bit].reshape(total * 2, bit),
+        jnp.concatenate([held[:, :bit], held[:, bit:]], axis=0),
+        (((1,), (1,)), ((), ())),
+        preferred_element_type=jnp.float32,
+    ).reshape(n, 2, rows, 2 * LANES)
+    slot_of = arrived[:, :, bit:].astype(jnp.float32).reshape(n, 2, rows, LANES)[:, 0]
+    adapter = lax.broadcasted_iota(jnp.int32, (n, rows, LANES), 2) // pair_rank + side * m
+    low = product[:, 0, :, :LANES] + product[:, 1, :, LANES:]
+    low = jnp.where(slot_of == adapter.astype(jnp.float32), low, 0.0)
+    sum_send[...] = low
+    sum_recv[seat] = sum_send[seat]
+    for other in seats:
+        sum_copy(other, seat).start()
+    for other in seats:
+        sum_copy(other, other).wait_recv()
+    codes[side, seat] = jnp.sum(sum_recv[...], axis=0)
+    everyone = [(peer, peer_core) for peer in across for peer_core in (core, 1 - core)]
+    everyone += [(peer, peer_core) for peer in beside for peer_core in (core, 1 - core)]
+    everyone += [(me, 1 - core)]
+    for peer, peer_core in everyone:
+        code_copy(peer, peer_core, side, seat).start()
+
+    def stacked(values):
+        lane = lax.broadcasted_iota(jnp.int32, values.shape, 2)
+        is_gate = lax.rem(lane, pair_rank) < pair_rank // 2
+        both = [jnp.where(is_gate, values, 0.0), jnp.where(is_gate, 0.0, values)]
+        return jnp.stack(both, axis=1).reshape(2 * total, values.shape[2]).astype(jnp.bfloat16)
+
+    for other in seats:
+        code_copy(side * m + other // 2, lax.rem(other, 2), side, other).wait_recv()
+    near_codes = stacked(codes[side])
+    loads[2].wait()
+    for peer in beside:
+        near_copy(peer, lax.rem(peer, m)).wait_recv()
+
+    def expand(which, spread):
+        kind, start, size = parts[which]
+        source, send = (near_up, near_send) if kind else (wide_up, wide_send)
+        columns = pl.ds(start, size)
+        depth = spread.shape[1]
+        delta = jnp.dot(
+            spread,
+            source[:, :, columns].reshape(depth, size),
+            preferred_element_type=jnp.float32,
+        )
+        send[:, :, columns] = delta.astype(jnp.bfloat16).reshape(n, 2 * rows, size)
+        for peer in peers:
+            back_copy(peer, me, which).start()
+
+    for which, (kind, _, _) in enumerate(parts):
+        if kind:
+            expand(which, near_codes)
+
+    for other in range(n):
+        code_copy((1 - side) * m + other // 2, other % 2, 1 - side, other).wait_recv()
+    wide_codes = stacked(jnp.concatenate([codes[0], codes[1]], axis=2))
+    loads[1].wait()
+    for peer in peers:
+        wide_copy(peer, peer).wait_recv()
+    for which, (kind, _, _) in enumerate(parts):
+        if not kind:
+            expand(which, wide_codes)
+
+    loads[3].wait()
+    loads[4].wait()
+
+    def finish(start, size, block):
+        columns = span(start, size)
+        gate = gate_vmem[:, columns].astype(jnp.float32) + block[:rows]
+        raised = up_vmem[:, columns].astype(jnp.float32) + block[rows:]
+        out[:, columns] = (jax.nn.silu(gate) * raised).astype(out.dtype)
+
+    for which, (kind, start, size) in enumerate(parts):
+        columns = pl.ds(start, size)
+        if kind:
+            for step in range(m):
+                spot = lax.rem(place + step, m)
+                if step:
+                    mine = side * m + spot
+                    back_copy(mine, mine, which).wait_recv()
+                    own = near_recv[mine, :, columns]
+                else:
+                    own = near_send[me, :, columns]
+                far = (1 - side) * m + spot
+                back_copy(far, far, which).wait_recv()
+                block = own.astype(jnp.float32) + near_recv[far, :, columns].astype(jnp.float32)
+                finish(wide_total + spot * near + start, size, block)
+        else:
+            own = wide_send[me, :, columns].astype(jnp.float32)
+            finish(me * wide + start, size, own)
+            for peer in beside + across:
+                back_copy(peer, peer, which).wait_recv()
+                block = wide_recv[peer, :, columns].astype(jnp.float32)
+                finish(peer * wide + start, size, block)
+
+    for peer in peers:
+        tok_copy(peer, me).wait_send()
+        wide_copy(peer, me).wait_send()
+        for which in range(len(parts)):
+            back_copy(peer, me, which).wait_send()
+    for peer in beside:
+        down_copy(peer, place).wait_send()
+        near_copy(peer, place).wait_send()
+    for other in seats:
+        sum_copy(other, seat).wait_send()
+    for peer, peer_core in everyone:
+        code_copy(peer, peer_core, side, seat).wait_send()
+
+
+def cut(size, pieces):
+    tiles = size // LANES
+    edges = [tiles * k // pieces * LANES for k in range(pieces + 1)]
+    return [(a, b - a) for a, b in zip(edges, edges[1:]) if b > a]
+
+
+WIDE_TILES = 6
+NEAR_PIECES = 2
+WIDE_PIECES = 1
+
+
+def local(mesh, *arrays):
+    tokens, ids, storage, down, up, gate_base, up_base = arrays
+    n = mesh.shape["dp"]
+    rows, width = tokens.shape
+    held, pair_rank, _ = down.shape
+    hidden = up.shape[2]
+    m = n // 2
+    wide = WIDE_TILES * LANES
+    near = (hidden - n * wide) // m
+    fits = (
+        held == 1
+        and n % 2 == 0
+        and n == rows == 8
+        and mesh.shape["tensor"] == 2
+        and m * pair_rank == LANES
+        and width % (2 * m * LANES) == 0
+        and near > 0
+        and near % LANES == 0
+        and n * wide + m * near == hidden
+    )
+    if not fits:
+        return plain(*arrays)
+    parts = [(1, *edge) for edge in cut(near, NEAR_PIECES)]
+    parts += [(0, *edge) for edge in cut(wide, WIDE_PIECES)]
+    count = len(parts)
+    vmem = pl.BlockSpec(memory_space=pltpu.VMEM)
+    smem = pl.BlockSpec(memory_space=pltpu.SMEM)
+    hbm = pl.BlockSpec(memory_space=pl.ANY)
+    dma = pltpu.SemaphoreType.DMA
+    bf16 = jnp.bfloat16
+    packed = width // (2 * m) + LANES
+    return pl.pallas_call(
+        functools.partial(kernel, n, parts),
+        out_shape=jax.ShapeDtypeStruct((rows, hidden), bf16),
+        in_specs=[smem, smem, hbm, hbm, hbm, hbm, hbm],
+        out_specs=vmem,
+        scratch_shapes=[
+            pltpu.VMEM((rows, width), bf16),
+            pltpu.VMEM((m, 2 * rows, packed), bf16),
+            pltpu.VMEM((n, 2 * rows, packed), bf16),
+            pltpu.VMEM((m, pair_rank, width // m), bf16),
+            pltpu.VMEM((n, rows, LANES), jnp.float32),
+            pltpu.VMEM((n, rows, LANES), jnp.float32),
+            pltpu.VMEM((2, n, rows, LANES), jnp.float32),
+            pltpu.VMEM((n, pair_rank, wide), bf16),
+            pltpu.VMEM((m, pair_rank, near), bf16),
+            pltpu.VMEM((n, 2 * rows, wide), bf16),
+            pltpu.VMEM((n, 2 * rows, near), bf16),
+            pltpu.VMEM((n, 2 * rows, wide), bf16),
+            pltpu.VMEM((n, 2 * rows, near), bf16),
+            pltpu.VMEM((rows, hidden), bf16),
+            pltpu.VMEM((rows, hidden), bf16),
+            dma((n,)),
+            dma((n,)),
+            dma((m,)),
+            dma((m,)),
+            dma((n,)),
+            dma((n,)),
+            dma((n, 2)),
+            dma((2, n)),
+            dma((n,)),
+            dma((n,)),
+            dma((m,)),
+            dma((m,)),
+            dma((n, count)),
+            dma((n, count)),
+            dma((6,)),
+        ],
+        compiler_params=pltpu.CompilerParams(
+            collective_id=0, has_side_effects=True, vmem_limit_bytes=60 * 1024 * 1024
+        ),
+    )(ids, storage, tokens, down[0], up[0], gate_base, up_base)
+
+
 def solution(mesh):
     in_specs = (
         P(("groups", "dp"), "tensor"),
@@ -82,4 +484,4 @@
         P(("groups", "dp"), "tensor"),
     )
     out_specs = P(("groups", "dp"), "tensor")
-    return jax.shard_map(local, mesh=mesh, in_specs=in_specs, out_specs=out_specs, check_vma=False)
+    return jax.shard_map(functools.partial(local, mesh), mesh=mesh, in_specs=in_specs, out_specs=out_specs, check_vma=False)

time: 140 us -> 51.6 us (0.37)
  blocking collectives: 124 us -> 0 us
  Pallas kernels: 0 us -> 49.8 us
  starting transfers between devices: 7.38 us -> 0 us
  local copies, waits for them, and re-layouts: 6.05 us -> 1.64 us
    psum x1 -> x0, blocking collectives: 57.6 us -> none  [local(): low_rank = lax.psum(term_rows, ('dp', 'tensor'))]
    pallas_call x0 -> x1, Pallas kernels: none -> 49.8 us  [local(): pl.pallas_call(functools.partial(kernel, n, parts), out_shape=jax.ShapeDt...]
    all_gather x1 -> x0, blocking collectives: 31.3 us -> none  [local(): shard_rows = lax.all_gather(tokens, 'dp', axis=0, tiled=True)]
    unnamed x1 -> x0, blocking collectives: 20.5 us -> none
    all_to_all x1 -> x0, blocking collectives: 14.3 us -> none  [local(): lax.all_to_all(deltas, 'dp', split_axis=0, concat_axis=2, tiled=True)]
    all_to_all x1 -> x0, starting transfers between devices: 7.38 us -> none  [local(): lax.all_to_all(adapter_up_weight.reshape(holding_count * paired_rank, ada...]
    unnamed x18 -> x1, local copies, waits for them, and re-layouts: 4.44 us -> 1.64 us
  transfers between devices with their start and end apart: 1 -> 0, of which waited for: 0 -> 0; matrix products, arithmetic and copies ran while one was open for 1% -> 0% of each run, Pallas kernels for 0% -> 0%
where the time goes in v2:
time: 51.6 us; the launch traced here: 51.5 us
  Pallas kernels  49.8 us (97%)
  local copies, waits for them, and re-layouts  1.64 us (3%)
    pallas_call x1, Pallas kernels, local(): pl.pallas_call(functools.partial(kernel, n, parts), out_shape=jax.ShapeDt...  49.8 us
    unnamed x1, local copies, waits for them, and re-layouts  1.64 us

profile of v2, /device:TPU:0, one launch (start us, length us, event | category | flops | bytes accessed | tf_op | source)
XLA Modules:
  0.0 51.5 jit_solution(9502480489933048349)
XLA Ops:
  0.0 49.8 %shard_map.73 = bf16[8,14336]{1,0:T(8,128)(2,1)} custom-call(s32[8]{0:T(128)} %ids.1, s32[8]{0:T(128)} %storage.1, bf16[8,4096]{1,0:T(8,128)(2,1)} %tokens.1, bf16[32,4096]{1,0:T(8,128)(2,1)} %bitcast.3, bf16[32,14336]{1,0:T(8,128)(2,1)} %bitcast.2, bf16[8,14336]{1,0:T(8,128)(2,1)} %gate_base.1, bf16[8,14336]{1,0:T(8,128)(2,1)} %up_base.1), custom_call_target="tpu_custom_call" | custom-call | tf_op jit(solution)/shard_map/pallas_call | solution.py:433
  49.8 1.6 %copy.9 = bf16[8,14336]{1,0:T(8,128)(2,1)} copy(bf16[8,14336]{1,0:T(8,128)(2,1)} %shard_map.73) | data formatting | bytes 458752

commit v3 on v2

--- a/solution.py
+++ b/solution.py
@@ -81,14 +81,16 @@
 def kernel(
     n,
     parts,
-    ids,
-    storage,
+    ids_hbm,
+    storage_hbm,
     tokens,
     down,
     up,
     gate_base,
     up_base,
     out,
+    ids,
+    storage,
     tok_vmem,
     tok_send,
     tok_all,
@@ -151,6 +153,12 @@
 
     tok_load = pltpu.make_async_copy(tokens, tok_vmem, local_sem.at[0])
     tok_load.start()
+    index_loads = [
+        pltpu.make_async_copy(ids_hbm, ids, local_sem.at[6]),
+        pltpu.make_async_copy(storage_hbm, storage, local_sem.at[7]),
+    ]
+    for copy in index_loads:
+        copy.start()
     barrier = pltpu.get_barrier_semaphore()
     for peer in peers:
         for peer_core in range(2):
@@ -174,6 +182,8 @@
     for copy in loads:
         copy.start()
 
+    for copy in index_loads:
+        copy.wait()
     slot_rows = lax.broadcasted_iota(jnp.int32, (rows, LANES), 0)
     slots = jnp.zeros((rows, LANES), jnp.int32)
     for row in range(rows):
@@ -264,18 +274,26 @@
         tok_copy(peer, me).start()
     for peer in beside:
         down_copy(peer, place).start()
-    for peer in across:
-        wide_copy(peer, me).start()
-    for peer in beside:
-        near_copy(peer, place).start()
-    for peer in beside:
-        wide_copy(peer, me).start()
+
+    def send_up(moment):
+        for peer, when in zip(across, WIDE_ACROSS):
+            if when == moment:
+                wide_copy(peer, me).start()
+        for peer, when in zip(beside, NEAR_BESIDE):
+            if when == moment:
+                near_copy(peer, place).start()
+        for peer, when in zip(beside, WIDE_BESIDE):
+            if when == moment:
+                wide_copy(peer, me).start()
+
+    send_up(0)
 
     loads[0].wait()
     for peer in beside:
         down_copy(peer, lax.rem(peer, m)).wait_recv()
     for peer in peers:
         tok_copy(peer, peer).wait_recv()
+    send_up(1)
     arrived = tok_all[...]
     held = down_all[...].reshape(m * pair_rank, piece)
     product = lax.dot_general(
@@ -292,6 +310,7 @@
     sum_recv[seat] = sum_send[seat]
     for other in seats:
         sum_copy(other, seat).start()
+    send_up(2)
     for other in seats:
         sum_copy(other, other).wait_recv()
     codes[side, seat] = jnp.sum(sum_recv[...], axis=0)
@@ -300,6 +319,7 @@
     everyone += [(me, 1 - core)]
     for peer, peer_core in everyone:
         code_copy(peer, peer_core, side, seat).start()
+    send_up(3)
 
     def stacked(values):
         lane = lax.broadcasted_iota(jnp.int32, values.shape, 2)
@@ -325,8 +345,11 @@
             preferred_element_type=jnp.float32,
         )
         send[:, :, columns] = delta.astype(jnp.bfloat16).reshape(n, 2 * rows, size)
-        for peer in peers:
+        for peer in across:
             back_copy(peer, me, which).start()
+        if not LATE_BESIDE:
+            for peer in beside:
+                back_copy(peer, me, which).start()
 
     for which, (kind, _, _) in enumerate(parts):
         if kind:
@@ -342,6 +365,10 @@
         if not kind:
             expand(which, wide_codes)
 
+    if LATE_BESIDE:
+        for which in range(len(parts)):
+            for peer in beside:
+                back_copy(peer, me, which).start()
     loads[3].wait()
     loads[4].wait()
 
@@ -394,8 +421,12 @@
     return [(a, b - a) for a, b in zip(edges, edges[1:]) if b > a]
 
 
-WIDE_TILES = 6
-NEAR_PIECES = 2
+WIDE_ACROSS = (0, 0, 2, 3)
+NEAR_BESIDE = (0, 0, 2)
+WIDE_BESIDE = (3, 3, 3)
+LATE_BESIDE = 0
+WIDE_TILES = 10
+NEAR_PIECES = 1
 WIDE_PIECES = 1
 
 
@@ -425,7 +456,6 @@
     parts += [(0, *edge) for edge in cut(wide, WIDE_PIECES)]
     count = len(parts)
     vmem = pl.BlockSpec(memory_space=pltpu.VMEM)
-    smem = pl.BlockSpec(memory_space=pltpu.SMEM)
     hbm = pl.BlockSpec(memory_space=pl.ANY)
     dma = pltpu.SemaphoreType.DMA
     bf16 = jnp.bfloat16
@@ -433,9 +463,11 @@
     return pl.pallas_call(
         functools.partial(kernel, n, parts),
         out_shape=jax.ShapeDtypeStruct((rows, hidden), bf16),
-        in_specs=[smem, smem, hbm, hbm, hbm, hbm, hbm],
+        in_specs=[hbm, hbm, hbm, hbm, hbm, hbm, hbm],
         out_specs=vmem,
         scratch_shapes=[
+            pltpu.SMEM(ids.shape, ids.dtype),
+            pltpu.SMEM(storage.shape, storage.dtype),
             pltpu.VMEM((rows, width), bf16),
             pltpu.VMEM((m, 2 * rows, packed), bf16),
             pltpu.VMEM((n, 2 * rows, packed), bf16),
@@ -465,7 +497,7 @@
             dma((m,)),
             dma((n, count)),
             dma((n, count)),
-            dma((6,)),
+            dma((8,)),
         ],
         compiler_params=pltpu.CompilerParams(
             collective_id=0, has_side_effects=True, vmem_limit_bytes=60 * 1024 * 1024

time: 51.6 us -> 43.6 us (0.84)
  Pallas kernels: 49.8 us -> 41.8 us
    pallas_call x1, Pallas kernels: 49.8 us -> 41.8 us  [local(): pl.pallas_call(functools.partial(kernel, n, parts), out_shape=jax.ShapeDt...]
where the time goes in v3:
time: 43.6 us; the launch traced here: 43.4 us
  Pallas kernels  41.8 us (96%)
  local copies, waits for them, and re-layouts  1.64 us (4%)
    pallas_call x1, Pallas kernels, local(): pl.pallas_call(functools.partial(kernel, n, parts), out_shape=jax.ShapeDt...  41.8 us
    unnamed x1, local copies, waits for them, and re-layouts  1.64 us

profile of v3, /device:TPU:0, one launch (start us, length us, event | category | flops | bytes accessed | tf_op | source)
XLA Modules:
  0.0 43.4 jit_solution(4224475939085046240)
XLA Ops:
  0.0 41.8 %shard_map.73 = bf16[8,14336]{1,0:T(8,128)(2,1)} custom-call(s32[8]{0:T(128)} %ids_hbm.1, s32[8]{0:T(128)} %storage_hbm.1, bf16[8,4096]{1,0:T(8,128)(2,1)} %tokens.1, bf16[32,4096]{1,0:T(8,128)(2,1)} %bitcast.3, bf16[32,14336]{1,0:T(8,128)(2,1)} %bitcast.2, bf16[8,14336]{1,0:T(8,128)(2,1)} %gate_base.1, bf16[8,14336]{1,0:T(8,128)(2,1)} %up_base.1), custom_call_target="tpu_custom_call" | custom-call | tf_op jit(solution)/shard_map/pallas_call | solution.py:463
  41.8 1.6 %copy.9 = bf16[8,14336]{1,0:T(8,128)(2,1)} copy(bf16[8,14336]{1,0:T(8,128)(2,1)} %shard_map.73) | data formatting | bytes 458752

commit v4 on v3

--- a/solution.py
+++ b/solution.py
@@ -88,7 +88,9 @@
     up,
     gate_base,
     up_base,
+    out_hbm,
     out,
+    out_sem,
     ids,
     storage,
     tok_vmem,
@@ -372,11 +374,19 @@
     loads[3].wait()
     loads[4].wait()
 
+    stores = []
+
     def finish(start, size, block):
         columns = span(start, size)
         gate = gate_vmem[:, columns].astype(jnp.float32) + block[:rows]
         raised = up_vmem[:, columns].astype(jnp.float32) + block[rows:]
         out[:, columns] = (jax.nn.silu(gate) * raised).astype(out.dtype)
+        stores.append(
+            pltpu.make_async_copy(
+                out.at[:, columns], out_hbm.at[:, columns], out_sem.at[len(stores)]
+            )
+        )
+        stores[-1].start()
 
     for which, (kind, start, size) in enumerate(parts):
         columns = pl.ds(start, size)
@@ -401,6 +411,8 @@
                 block = wide_recv[peer, :, columns].astype(jnp.float32)
                 finish(peer * wide + start, size, block)
 
+    for copy in stores:
+        copy.wait()
     for peer in peers:
         tok_copy(peer, me).wait_send()
         wide_copy(peer, me).wait_send()
@@ -455,7 +467,6 @@
     parts = [(1, *edge) for edge in cut(near, NEAR_PIECES)]
     parts += [(0, *edge) for edge in cut(wide, WIDE_PIECES)]
     count = len(parts)
-    vmem = pl.BlockSpec(memory_space=pltpu.VMEM)
     hbm = pl.BlockSpec(memory_space=pl.ANY)
     dma = pltpu.SemaphoreType.DMA
     bf16 = jnp.bfloat16
@@ -464,8 +475,10 @@
         functools.partial(kernel, n, parts),
         out_shape=jax.ShapeDtypeStruct((rows, hidden), bf16),
         in_specs=[hbm, hbm, hbm, hbm, hbm, hbm, hbm],
-        out_specs=vmem,
+        out_specs=hbm,
         scratch_shapes=[
+            pltpu.VMEM((rows, hidden), bf16),
+            dma((count * n,)),
             pltpu.SMEM(ids.shape, ids.dtype),
             pltpu.SMEM(storage.shape, storage.dtype),
             pltpu.VMEM((rows, width), bf16),

time: 43.6 us -> 43.6 us (level)
  no operation moved by 1% of the time
where the time goes in v4:
time: 43.6 us; the launch traced here: 43.5 us
  Pallas kernels  41.8 us (96%)
  local copies, waits for them, and re-layouts  1.64 us (4%)
    pallas_call x1, Pallas kernels, local(): pl.pallas_call(functools.partial(kernel, n, parts), out_shape=jax.ShapeDt...  41.8 us
    unnamed x1, local copies, waits for them, and re-layouts  1.64 us

profile of v4, /device:TPU:0, one launch (start us, length us, event | category | flops | bytes accessed | tf_op | source)
XLA Modules:
  0.0 43.5 jit_solution(12522819634520349159)
XLA Ops:
  0.0 41.8 %shard_map.73 = bf16[8,14336]{1,0:T(8,128)(2,1)} custom-call(s32[8]{0:T(128)} %ids_hbm.1, s32[8]{0:T(128)} %storage_hbm.1, bf16[8,4096]{1,0:T(8,128)(2,1)} %tokens.1, bf16[32,4096]{1,0:T(8,128)(2,1)} %bitcast.3, bf16[32,14336]{1,0:T(8,128)(2,1)} %bitcast.2, bf16[8,14336]{1,0:T(8,128)(2,1)} %gate_base.1, bf16[8,14336]{1,0:T(8,128)(2,1)} %up_base.1), custom_call_target="tpu_custom_call" | custom-call | tf_op jit(solution)/shard_map/pallas_call | solution.py:474
  41.8 1.6 %copy.9 = bf16[8,14336]{1,0:T(8,128)(2,1)} copy(bf16[8,14336]{1,0:T(8,128)(2,1)} %shard_map.73) | data formatting | bytes 458752
